TPU v7x, 32 devices: a whole 2x2x4 slice. The times are simulated.
32 devices in a mesh: parts: 2 (over y), replica: 4 (over z), tensor: 4 (over x, core).
Axes of the slice: x: 2, y: 2, z: 4, core: 2. Of those that a mesh axis runs over, the one named last changes fastest.
Arguments:
- attention_rows: bfloat16 [2048, 8192], P(('parts', 'replica'), 'tensor'), parts along dimension 0, may hold values from -6 to 6
- output_projection_weight: bfloat16 [8192, 8192], P('tensor', 'replica'), may hold values from -0.0625 to 0.0625
- adapter_down_factors: bfloat16 [256, 16, 8192], P('replica', None, 'tensor'), may hold values from -0.0625 to 0.0625
- adapter_up_factors: bfloat16 [256, 16, 8192], P('tensor', None, 'replica'), may hold values from -1.5 to 1.5
- row_segment_slot: int32 [2048], P('parts'), parts along dimension 0, may hold values from 0 to 15, as said below
- segment_slot_adapter: int32 [8, 16], P('parts'), parts along dimension 0, may hold values from -1 to 255, as said below
Outputs:
- projected: bfloat16 [2048, 8192], P(('parts', 'tensor'), 'replica'), parts along dimension 0
There are 2 independent parts, one for each index of `parts`. A program takes and returns all parts, laid end to end along the dimension named above; an argument that names none is the same for every part. Nothing has to cross between parts.
Inputs may be any that keep to these rules, and one draw needn't show every extreme that they name: row_segment_slot[i] names a slot of row i // 256 of segment_slot_adapter that is not -1; when 256 is at least the number of such slots, every one of them is named by some row of that group. `segment_slot_adapter`: in each row g, slots o * 4 to o * 4 + 3 hold distinct adapters of o * 64 to (o + 1) * 64 - 1, filled slots first, then -1; in every draw some owner o has all 4 slots filled in every row, and every row has some owner with all 4 slots filled.
All inputs are finite; a program needn't handle non-finite values.
Results may differ from a plain program's by a relative error of at most 0.0065.
Values may be sent and summed in bfloat16 or wider, within the bound.
A program may use at most 128 MiB of HBM per device.

v0:
```python
import jax
import jax.numpy as jnp
from jax import lax
from jax.sharding import PartitionSpec as P

adapter_scale = 2.0


def owner_rows(table, owner, groups, owned_adapter_count):
    wanted = table.reshape(groups, groups, table.shape[1] // groups)
    mine_ids = lax.dynamic_index_in_dim(wanted, owner, 1, keepdims=False)
    return jnp.clip(mine_ids - owner * owned_adapter_count, 0, owned_adapter_count - 1)


def slot_select(slot_block, slot_count):
    return slot_block[:, None] == jnp.arange(slot_count, dtype=jnp.int32)[None, :]


def per_device(
    attention_rows,
    output_projection_weight,
    adapter_down_factors,
    adapter_up_factors,
    row_segment_slot,
    segment_slot_adapter,
):
    groups = lax.axis_size("replica")
    owned_adapter_count = adapter_down_factors.shape[0]
    slot_count = segment_slot_adapter.shape[1]
    rank_extent = adapter_down_factors.shape[1]
    row_count = attention_rows.shape[0]
    replica_pos = lax.axis_index("replica")
    tensor_pos = lax.axis_index("tensor")
    down_adapter_index = owner_rows(segment_slot_adapter, replica_pos, groups, owned_adapter_count)
    down_factor_outgoing = jnp.take(adapter_down_factors, down_adapter_index, axis=0)
    down_got = lax.all_to_all(
        down_factor_outgoing, "replica", split_axis=0, concat_axis=0, tiled=True
    )
    down_flat = down_got.reshape(slot_count * rank_extent, down_got.shape[-1])
    every_slot = lax.dot_general(
        attention_rows, down_flat, (((1,), (1,)), ((), ())), preferred_element_type=jnp.float32
    )
    own_slots = lax.dynamic_slice_in_dim(row_segment_slot, replica_pos * row_count, row_count, 0)
    pick_rows = slot_select(own_slots, slot_count).astype(jnp.float32)
    shrink_part = jnp.sum(
        every_slot.reshape(row_count, slot_count, rank_extent) * pick_rows[:, :, None], axis=1
    )
    shrink_local = lax.psum(shrink_part, "tensor").astype(jnp.bfloat16)
    gathered, shrink_all = (
        lax.all_gather(attention_rows, "replica", axis=0, tiled=True),
        lax.all_gather(shrink_local, "replica", axis=0, tiled=True),
    )
    base_output = lax.psum_scatter(
        jnp.dot(gathered, output_projection_weight, preferred_element_type=jnp.float32).astype(
            jnp.bfloat16
        ),
        "tensor",
        scatter_dimension=0,
        tiled=True,
    ).astype(jnp.float32)
    up_adapter_index = owner_rows(segment_slot_adapter, tensor_pos, groups, owned_adapter_count)
    up_factor_outgoing = jnp.take(adapter_up_factors, up_adapter_index, axis=0)
    up_got = lax.all_to_all(up_factor_outgoing, "tensor", split_axis=0, concat_axis=0, tiled=True)
    target_slots = lax.dynamic_slice_in_dim(row_segment_slot, tensor_pos * row_count, row_count, 0)
    target_pick = slot_select(target_slots, slot_count).astype(jnp.bfloat16)
    mine_rows = lax.dynamic_slice_in_dim(shrink_all, tensor_pos * row_count, row_count, 0)
    spread = (target_pick[:, :, None] * mine_rows[:, None, :]).reshape(
        row_count, slot_count * rank_extent
    )
    adapter_delta = jnp.dot(
        spread,
        up_got.reshape(slot_count * rank_extent, up_got.shape[-1]),
        preferred_element_type=jnp.float32,
    )
    return (base_output + adapter_scale * adapter_delta).astype(jnp.bfloat16)


def solution(mesh):
    return jax.shard_map(
        per_device,
        mesh=mesh,
        in_specs=(
            P(("parts", "replica"), "tensor"),
            P("tensor", "replica"),
            P("replica", None, "tensor"),
            P("tensor", None, "replica"),
            P("parts"),
            P("parts", None),
        ),
        out_specs=P(("parts", "tensor"), "replica"),
        check_vma=False,
    )
```

profile of v0, /device:TPU:0, one launch (start us, length us, event | category | flops | bytes accessed | tf_op | source)
XLA Modules:
  0.0 187.9 jit_solution(16267511634327019814)
XLA Ops:
  6.5 0.0 all-gather.2.cloned.1.call-start
  6.5 0.7 all-gather.2.cloned.1.call-update
  7.3 0.0 reduce-scatter.2.cloned.1.call-start
  7.3 85.1 %all-gather.2.cloned.1.call-done = bf16[1024,2048]{1,0:T(8,128)(2,1)} async-done(((bf16[256,2048]{1,0:T(8,128)(2,1)}), bf16[1024,2048]{1,0:T(8,128)(2,1)}) %all-gather.2.cloned.1.call-update) | async-done | bytes 4194320 | tf_op jit(solution)/shard_map/all_gather | solution.py:50
  92.4 13.8 %convolution_convert_fusion = bf16[1024,2048]{1,0:T(8,128)(2,1)} fusion(bf16[1024,2048]{1,0:T(8,128)(2,1)} %all-gather.2.cloned.1.call-done, bf16[2048,2048]{1,0:T(8,128)(2,1)} %param.9), kind=kOutput, calls=%fused_computation.2 | convolution fusion | flops 8592031744 | bytes 16777216 | tf_op jit(solution)/shard_map/dot_general | solution.py:54
  106.2 0.0 copy-start.1
  106.2 0.0 reduce-scatter.2.cloned.1.call-update
  106.2 0.6 copy-done.1
  106.9 0.1 reshape.86
  107.0 0.1 reshape.110
  107.1 0.0 copy-start.2
  107.1 2.8 %gather_fusion = bf16[16,16,2048]{2,1,0:T(8,128)(2,1)S(1)} fusion(bf16[64,16,2048]{2,1,0:T(8,128)(2,1)} %param.10, s32[1024]{0:T(1024)S(1)} %pad_clamp_fusion.1), kind=kCustom, calls=%fused_computation.clone | custom fusion | bytes 2097216 | tf_op jit(solution)/shard_map/jit(_take)/gather | solution.py:35
  109.9 1.1 broadcast_select_fusion.1
  111.1 0.0 copy-start
  111.1 3.8 %all-to-all-start = ((bf16[4,4,16,2048]{3,2,1,0:T(8,128)(2,1)}), bf16[4,4,16,2048]{3,2,1,0:T(8,128)(2,1)S(1)}, u32[]{:S(2)}, u32[]{:S(2)}) async-start(bf16[4,4,16,2048]{3,2,1,0:T(8,128)(2,1)} %broadcast_select_fusion.1), calls=%async_computation.1 | async-start | bytes 2097152 | tf_op jit(solution)/shard_map/all_to_all | solution.py:36
  114.9 0.1 reshape.114
  115.0 3.0 %gather_fusion.1 = bf16[16,16,2048]{2,1,0:T(8,128)(2,1)S(1)} fusion(bf16[64,16,2048]{2,1,0:T(8,128)(2,1)} %param.11, s32[1024]{0:T(1024)S(1)} %pad_clamp_fusion), kind=kCustom, calls=%fused_computation.1.clone | custom fusion | bytes 2097216 | tf_op jit(solution)/shard_map/jit(_take)/gather | solution.py:62
  118.0 0.0 copy-done.2
  118.0 0.1 fusion.4
  118.1 1.2 broadcast_select_fusion
  119.2 21.5 %all-to-all-done = bf16[4,4,16,2048]{3,2,1,0:T(8,128)(2,1)S(1)} async-done(((bf16[4,4,16,2048]{3,2,1,0:T(8,128)(2,1)}), bf16[4,4,16,2048]{3,2,1,0:T(8,128)(2,1)S(1)}, u32[]{:S(2)}, u32[]{:S(2)}) %all-to-all-start) | async-done | bytes 1048608 | tf_op jit(solution)/shard_map/all_to_all | solution.py:36
  140.8 3.5 %all-to-all-start.1 = ((bf16[4,4,16,2048]{3,2,1,0:T(8,128)(2,1)}), bf16[4,4,16,2048]{3,2,1,0:T(8,128)(2,1)S(1)}, u32[]{:S(2)}, u32[]{:S(2)}) async-start(bf16[4,4,16,2048]{3,2,1,0:T(8,128)(2,1)} %broadcast_select_fusion), calls=%async_computation.2 | async-start | bytes 2097152 | tf_op jit(solution)/shard_map/all_to_all | solution.py:63
  144.3 0.0 copy-done
  144.3 0.5 fusion.5
  144.8 20.1 %psum.7 = bf16[256,16]{0,1:T(8,128)(2,1)S(1)} all-reduce(f32[256,16]{0,1:T(8,128)S(1)} %multiply_reduce_fusion), channel_id=1, replica_groups=mesh['parts'=2,'replica'=4,'tensor'=4] {'tensor'}, use_global_device_ids=true, to_apply=%region_2.4 | all-reduce | flops 4096 | bytes 24576 | tf_op jit(solution)/shard_map/psum | solution.py:48
  165.0 13.4 %all_gather.7 = bf16[1024,16]{0,1:T(8,128)(2,1)S(1)} all-gather(bf16[256,16]{0,1:T(8,128)(2,1)S(1)} %psum.7), channel_id=1, replica_groups=mesh['parts'=2,'replica'=4,'tensor'=4] {'replica'}, dimensions={0}, use_global_device_ids=true | all-gather | bytes 40960 | tf_op jit(solution)/shard_map/all_gather | solution.py:51
  178.4 0.0 all-to-all-done.1
  178.4 0.0 reduce-scatter.2.cloned.1.call-done
  178.4 2.7 %fusion.1 = bf16[256,2048]{1,0:T(8,128)(2,1)} fusion(bf16[256,256]{0,1:T(8,128)(2,1)S(1)} %bitcast.21, bf16[256,2048]{1,0:T(8,128)(2,1)S(1)} %bitcast.16, bf16[256,2048]{1,0:T(8,128)(2,1)} %reduce-scatter.2.cloned.1.call-done), kind=kOutput, calls=%fused_computation.5 | convolution fusion | flops 270532608 | bytes 3276800 | tf_op jit(solution)/shard_map/dot_general | solution.py:70
  (12 shorter events, 0.1 us)
Async XLA Ops:
  6.5 85.9 %all-gather.2.cloned.1.call-start = ((), (), s32[]{:S(2)}) async-start(), calls=%async_computation.3 | async-start | bytes 5242880 | tf_op jit(solution)/shard_map/all_gather | solution.py:50
  7.3 171.2 %reduce-scatter.2.cloned.1.call-start = ((), (), s32[]{:S(2)}) async-start(), calls=%async_computation.4 | async-start | bytes 5242880 | tf_op jit(solution)/shard_map/reduce_scatter | solution.py:53
  106.2 0.7 copy-start.1
  107.1 10.9 %copy-start.2 = (s32[1024]{0:T(1024)S(1)}, s32[1024]{0:T(1024)}, u32[]{:S(2)}) copy-start(s32[1024]{0:T(1024)} %param.12) | copy-start | bytes 12292
  111.1 33.2 %copy-start = (bf16[256,2048]{1,0:T(8,128)(2,1)S(1)}, bf16[256,2048]{1,0:T(8,128)(2,1)}, u32[]{:S(2)}) copy-start(bf16[256,2048]{1,0:T(8,128)(2,1)} %param.8) | copy-start | bytes 3145732
  111.1 29.7 %all-to-all-start = ((bf16[4,4,16,2048]{3,2,1,0:T(8,128)(2,1)}), bf16[4,4,16,2048]{3,2,1,0:T(8,128)(2,1)S(1)}, u32[]{:S(2)}, u32[]{:S(2)}) async-start(bf16[4,4,16,2048]{3,2,1,0:T(8,128)(2,1)} %broadcast_select_fusion.1), calls=%async_computation.1 | async-start | bytes 2097152 | tf_op jit(solution)/shard_map/all_to_all | solution.py:36
  140.8 37.6 %all-to-all-start.1 = ((bf16[4,4,16,2048]{3,2,1,0:T(8,128)(2,1)}), bf16[4,4,16,2048]{3,2,1,0:T(8,128)(2,1)S(1)}, u32[]{:S(2)}, u32[]{:S(2)}) async-start(bf16[4,4,16,2048]{3,2,1,0:T(8,128)(2,1)} %broadcast_select_fusion), calls=%async_computation.2 | async-start | bytes 2097152 | tf_op jit(solution)/shard_map/all_to_all | solution.py:63
Sparse Core Ops, SparseCore 0:
  8.9 83.4 all-gather.1
  106.4 43.6 reduce-scatter.1
where the time goes:
time: 188 us
  waiting for transfers between devices  107 us (57%)
  blocking collectives  33.5 us (18%)
  matrix products  16.9 us (9%)
  between operations  13.5 us (7%)
  starting transfers between devices  7.32 us (4%)
  local copies, waits for them, and re-layouts  6.81 us (4%)
  other arithmetic  2.42 us (1%)
    all_gather x1, waiting for transfers between devices, per_device(): lax.all_gather(attention_rows, 'replica', axis=0, tiled=True)  85.1 us
    all_to_all x1, waiting for transfers between devices, per_device(): lax.all_to_all(down_factor_outgoing, 'replica', split_axis=0, concat_axis...  21.5 us
    psum x1, blocking collectives, per_device(): shrink_local = lax.psum(shrink_part, 'tensor').astype(jnp.bfloat16)  20.1 us
    dot_general x1, matrix products, per_device(): jnp.dot(gathered, output_projection_weight, preferred_element_type=jnp.fl...  13.8 us
    all_gather x1, blocking collectives, per_device(): lax.all_gather(shrink_local, 'replica', axis=0, tiled=True)  13.4 us
    all_to_all x1, starting transfers between devices, per_device(): lax.all_to_all(down_factor_outgoing, 'replica', split_axis=0, concat_axis...  3.77 us
  transfers between devices with their start and end apart: 4, of which 2 were waited for; matrix products, arithmetic and copies ran while one was open for 5% of the time, Pallas kernels for 0%

commit v1 on v0

v1 whole, which is shorter than its diff:
```python
import functools

import jax
import jax.numpy as jnp
from jax import lax
from jax.experimental import pallas as pl
from jax.experimental.pallas import tpu as pltpu
from jax.sharding import PartitionSpec as P

MESH = pl.DeviceIdType.MESH
adapter_scale = 2.0
row_chunk = 64
tile_width = 1024


def kernel(
    groups, peers, chunks, tiles,
    table, slots, x_hbm, w_hbm, down_hbm, up_hbm,
    out,
    x_all, w_all, down, up, down_sel, up_send, up_got,
    share_out, share_got, rank_out, rank_got, fin_out, fin_got, delta,
    load_sem, x_right_sem, x_left_sem, x_recv_sem,
    up_send_sem, up_recv_sem, share_send_sem, share_recv_sem,
    rank_send_sem, rank_recv_sem, fin_send_sem, fin_recv_sem,
):
    z = lax.axis_index("replica")
    t = lax.axis_index("tensor")
    owned, rank, width = down.shape
    cap = table.shape[1] // groups
    rows = x_all.shape[2]

    barrier = pltpu.get_barrier_semaphore()
    for d in range(1, groups):
        pl.semaphore_signal(
            barrier, inc=1, device_id={"replica": lax.rem(z + d, groups)}, device_id_type=MESH
        )
    for d in range(1, peers):
        pl.semaphore_signal(
            barrier, inc=1, device_id={"tensor": lax.rem(t + d, peers)}, device_id_type=MESH
        )

    loads = [pltpu.make_async_copy(up_hbm, up, load_sem.at[0])]
    loads.append(pltpu.make_async_copy(down_hbm, down, load_sem.at[1]))
    loads.append(pltpu.make_async_copy(x_hbm, x_all.at[z], load_sem.at[2]))
    for i in range(tiles):
        loads.append(
            pltpu.make_async_copy(
                w_hbm.at[:, pl.ds(i * w_all.shape[2], w_all.shape[2])],
                w_all.at[i],
                load_sem.at[3 + i],
            )
        )
    for copy in loads:
        copy.start()
    pl.semaphore_wait(barrier, groups + peers - 2)

    def x_copy(src, g, c, step):
        sems = x_right_sem if step > 0 else x_left_sem
        return pltpu.make_async_remote_copy(
            src_ref=src,
            dst_ref=x_all.at[g, c],
            send_sem=sems.at[g, c],
            recv_sem=x_recv_sem.at[g, c],
            device_id={"replica": z + step},
            device_id_type=MESH,
        )

    for c in range(chunks):
        @pl.when(z < groups - 1)
        def _():
            x_copy(x_hbm.at[c], z, c, 1).start()

        @pl.when(z > 0)
        def _():
            x_copy(x_hbm.at[c], z, c, -1).start()

    def up_copy(g):
        return pltpu.make_async_remote_copy(
            src_ref=up_send.at[g],
            dst_ref=up_got.at[t],
            send_sem=up_send_sem.at[g],
            recv_sem=up_recv_sem.at[t],
            device_id={"tensor": g},
            device_id_type=MESH,
        )

    loads[0].wait()

    @pl.loop(0, peers)
    def _(g):
        for j in range(cap):
            index = jnp.clip(table[g, t * cap + j] - t * owned, 0, owned - 1)
            up_send[g, j * rank : (j + 1) * rank, :] = up[index]

        @pl.when(g != t)
        def _():
            up_copy(g).start()

        @pl.when(g == t)
        def _():
            up_got[t] = up_send[g]

    loads[1].wait()

    @pl.loop(0, groups)
    def _(g):
        for j in range(cap):
            index = jnp.clip(table[g, z * cap + j] - z * owned, 0, owned - 1)
            down_sel[g, j * rank : (j + 1) * rank, :] = down[index]

    for copy in loads[2:]:
        copy.wait()

    def share_copy(g, c, i):
        return pltpu.make_async_remote_copy(
            src_ref=share_out.at[g, c, i],
            dst_ref=share_got.at[t, c, i],
            send_sem=share_send_sem.at[g, c, i],
            recv_sem=share_recv_sem.at[t, c, i],
            device_id={"tensor": g},
            device_id_type=MESH,
        )

    def rank_copy(g):
        return pltpu.make_async_remote_copy(
            src_ref=rank_out.at[g],
            dst_ref=rank_got.at[t],
            send_sem=rank_send_sem.at[g],
            recv_sem=rank_recv_sem.at[t],
            device_id={"tensor": g},
            device_id_type=MESH,
        )

    def work(g, c):
        @pl.when(c == chunks - 1)
        def _():
            block = x_all[g].reshape(chunks * rows, width)
            terms = lax.dot_general(
                down_sel[g], block, (((1,), (1,)), ((), ())), preferred_element_type=jnp.float32
            )
            slot = slots[g]
            total = jnp.zeros((rank, chunks * rows), jnp.float32)
            for j in range(cap):
                total += jnp.where(slot == z * cap + j, terms[j * rank : (j + 1) * rank, :], 0.0)

            @pl.when(g == t)
            def _():
                rank_got[t] = total

            @pl.when(g != t)
            def _():
                rank_out[g] = total
                rank_copy(g).start()

        @pl.loop(0, tiles)
        def _(i):
            share = jnp.dot(
                x_all[g, c], w_all[i], preferred_element_type=jnp.float32
            ).astype(jnp.bfloat16)

            @pl.when(g == t)
            def _():
                share_got[t, c, i] = share

            @pl.when(g != t)
            def _():
                share_out[g, c, i] = share
                share_copy(g, c, i).start()

    @pl.loop(0, chunks)
    def _(c):
        work(z, c)

    @pl.loop(0, (groups - 1) * chunks)
    def _(e):
        s = e // chunks + 1
        c = lax.rem(e, chunks)
        low, high = z - s, z + s

        @pl.when(low >= 0)
        def _():
            x_copy(x_hbm.at[0], low, c, 1).wait_recv()

            @pl.when(z < groups - 1)
            def _():
                x_copy(x_all.at[low, c], low, c, 1).start()

        @pl.when(high < groups)
        def _():
            x_copy(x_hbm.at[0], high, c, -1).wait_recv()

            @pl.when(z > 0)
            def _():
                x_copy(x_all.at[high, c], high, c, -1).start()

        @pl.loop(0, 2)
        def _(side):
            g = z - s + side * 2 * s

            @pl.when((g >= 0) & (g < groups))
            def _():
                work(g, c)

    for d in range(1, peers):
        src = lax.rem(t + d, peers)
        pltpu.make_async_copy(rank_got.at[src], rank_got.at[src], rank_recv_sem.at[src]).wait()
    total = rank_got[0]
    for i in range(1, peers):
        total += rank_got[i]
    fin_out[...] = total.astype(jnp.bfloat16)
    fin_got[z] = total.astype(jnp.bfloat16)

    def fin_copy(d):
        return pltpu.make_async_remote_copy(
            src_ref=fin_out,
            dst_ref=fin_got.at[z],
            send_sem=fin_send_sem.at[d],
            recv_sem=fin_recv_sem.at[z],
            device_id={"replica": lax.rem(z + d, groups)},
            device_id_type=MESH,
        )

    for d in range(1, groups):
        fin_copy(d).start()
    for d in range(1, peers):
        src = lax.rem(t + d, peers)
        pltpu.make_async_copy(up_got.at[src], up_got.at[src], up_recv_sem.at[src]).wait()
    for d in range(1, groups):
        src = lax.rem(z + d, groups)
        pltpu.make_async_copy(fin_got.at[src], fin_got.at[src], fin_recv_sem.at[src]).wait()
    shrink = fin_got[0].astype(jnp.float32)
    for i in range(1, groups):
        shrink += fin_got[i].astype(jnp.float32)
    slot = slots[t]
    spread = jnp.concatenate(
        [jnp.where(slot == s, shrink, 0.0) for s in range(groups * cap)], axis=0
    ).astype(jnp.bfloat16)
    span = w_all.shape[2]
    for i in range(tiles):
        factors = up_got[:, :, i * span : (i + 1) * span].reshape(peers * cap * rank, span)
        delta[i] = adapter_scale * lax.dot_general(
            spread, factors, (((0,), (0,)), ((), ())), preferred_element_type=jnp.float32
        )

    for c in range(chunks):
        for i in range(tiles):
            for d in range(1, peers):
                src = lax.rem(t + d, peers)
                pltpu.make_async_copy(
                    share_got.at[src, c, i], share_got.at[src, c, i], share_recv_sem.at[src, c, i]
                ).wait()
            base = share_got[0, c, i].astype(jnp.float32)
            for p in range(1, peers):
                base += share_got[p, c, i].astype(jnp.float32)
            out[c * rows : (c + 1) * rows, i * span : (i + 1) * span] = (
                base + delta[i, c * rows : (c + 1) * rows, :]
            ).astype(jnp.bfloat16)

    @pl.loop(0, groups)
    def _(g):
        @pl.loop(0, chunks)
        def _(c):
            @pl.when((g <= z) & (z < groups - 1))
            def _():
                x_copy(x_all.at[g, c], g, c, 1).wait_send()

            @pl.when((g >= z) & (z > 0))
            def _():
                x_copy(x_all.at[g, c], g, c, -1).wait_send()

            @pl.when(g != t)
            def _():
                for i in range(tiles):
                    share_copy(g, c, i).wait_send()

        @pl.when(g != t)
        def _():
            rank_copy(g).wait_send()
            up_copy(g).wait_send()

    for d in range(1, groups):
        fin_copy(d).wait_send()


def per_device(
    attention_rows,
    output_projection_weight,
    adapter_down_factors,
    adapter_up_factors,
    row_segment_slot,
    segment_slot_adapter,
):
    groups = lax.axis_size("replica")
    peers = lax.axis_size("tensor")
    row_count, width = attention_rows.shape
    columns = output_projection_weight.shape[1]
    rank = adapter_down_factors.shape[1]
    slot_rows = (segment_slot_adapter.shape[1] // groups) * rank
    chunks = row_count // row_chunk
    span = min(tile_width, columns)
    tiles = columns // span
    rows = attention_rows.reshape(chunks, row_chunk, width)
    slots = row_segment_slot.reshape(groups, 1, row_count)
    dma = pltpu.SemaphoreType.DMA
    bf16 = jnp.bfloat16
    hbm = pl.BlockSpec(memory_space=pl.ANY)
    vmem = pl.BlockSpec(memory_space=pltpu.VMEM)
    return pl.pallas_call(
        functools.partial(kernel, groups, peers, chunks, tiles),
        out_shape=jax.ShapeDtypeStruct((row_count, columns), bf16),
        in_specs=[pl.BlockSpec(memory_space=pltpu.SMEM), vmem, hbm, hbm, hbm, hbm],
        out_specs=vmem,
        scratch_shapes=[
            pltpu.VMEM((groups, chunks, row_chunk, width), bf16),
            pltpu.VMEM((tiles, width, span), bf16),
            pltpu.VMEM(adapter_down_factors.shape, bf16),
            pltpu.VMEM(adapter_up_factors.shape, bf16),
            pltpu.VMEM((groups, slot_rows, width), bf16),
            pltpu.VMEM((peers, slot_rows, columns), bf16),
            pltpu.VMEM((peers, slot_rows, columns), bf16),
            pltpu.VMEM((peers, chunks, tiles, row_chunk, span), bf16),
            pltpu.VMEM((peers, chunks, tiles, row_chunk, span), bf16),
            pltpu.VMEM((peers, rank, row_count), jnp.float32),
            pltpu.VMEM((peers, rank, row_count), jnp.float32),
            pltpu.VMEM((rank, row_count), bf16),
            pltpu.VMEM((groups, rank, row_count), bf16),
            pltpu.VMEM((tiles, row_count, span), jnp.float32),
            dma((3 + tiles,)),
            dma((groups, chunks)),
            dma((groups, chunks)),
            dma((groups, chunks)),
            dma((peers,)),
            dma((peers,)),
            dma((peers, chunks, tiles)),
            dma((peers, chunks, tiles)),
            dma((peers,)),
            dma((peers,)),
            dma((groups,)),
            dma((groups,)),
        ],
        compiler_params=pltpu.CompilerParams(
            collective_id=0, has_side_effects=True, vmem_limit_bytes=56 * 1024 * 1024
        ),
    )(
        segment_slot_adapter,
        slots,
        rows,
        output_projection_weight,
        adapter_down_factors,
        adapter_up_factors,
    )


def solution(mesh):
    return jax.shard_map(
        per_device,
        mesh=mesh,
        in_specs=(
            P(("parts", "replica"), "tensor"),
            P("tensor", "replica"),
            P("replica", None, "tensor"),
            P("tensor", None, "replica"),
            P("parts"),
            P("parts", None),
        ),
        out_specs=P(("parts", "tensor"), "replica"),
        check_vma=False,
    )
```

time: 188 us -> 87.7 us (0.47)
  waiting for transfers between devices: 107 us -> 0 us
  Pallas kernels: 0 us -> 85.2 us
  blocking collectives: 33.5 us -> 0 us
  matrix products: 16.9 us -> 0 us
  between operations: 13.5 us -> 0.01 us
  starting transfers between devices: 7.32 us -> 0 us
  local copies, waits for them, and re-layouts: 6.81 us -> 2.3 us
  other arithmetic: 2.42 us -> 0 us
    pallas_call x0 -> x1, Pallas kernels: none -> 85.2 us  [per_device(): pl.pallas_call(functools.partial(kernel, groups, peers, chunks, tiles), o...]
    all_gather x1 -> x0, waiting for transfers between devices: 85.1 us -> none  [per_device(): lax.all_gather(attention_rows, 'replica', axis=0, tiled=True)]
    all_to_all x2 -> x0, waiting for transfers between devices: 21.5 us -> none  [the longest x1 21.5 us: per_device(): lax.all_to_all(down_factor_outgoing, 'replica', split_axis=0, concat_axis...]
    psum x1 -> x0, blocking collectives: 20.1 us -> none  [per_device(): shrink_local = lax.psum(shrink_part, 'tensor').astype(jnp.bfloat16)]
    dot_general x3 -> x0, matrix products: 16.9 us -> none  [the longest x1 13.8 us: per_device(): jnp.dot(gathered, output_projection_weight, preferred_element_type=jnp.fl...]
    all_gather x1 -> x0, blocking collectives: 13.4 us -> none  [per_device(): lax.all_gather(shrink_local, 'replica', axis=0, tiled=True)]
    all_to_all x2 -> x0, starting transfers between devices: 7.28 us -> none  [the longest x1 3.77 us: per_device(): lax.all_to_all(down_factor_outgoing, 'replica', split_axis=0, concat_axis...]
    gather x2 -> x0, local copies, waits for them, and re-layouts: 5.82 us -> none  [the longest x1 3 us: per_device(): up_factor_outgoing = jnp.take(adapter_up_factors, up_adapter_index, axis=0)]
  transfers between devices with their start and end apart: 4 -> 0, of which waited for: 2 -> 0; matrix products, arithmetic and copies ran while one was open for 5% -> 0% of each run, Pallas kernels for 0% -> 0%
where the time goes in v1:
time: 87.7 us; the launch traced here: 87.5 us
  Pallas kernels  85.2 us (97%)
  local copies, waits for them, and re-layouts  2.3 us (3%)
    pallas_call x1, Pallas kernels, per_device(): pl.pallas_call(functools.partial(kernel, groups, peers, chunks, tiles), o...  85.2 us
    unnamed x1, local copies, waits for them, and re-layouts  2.3 us

profile of v1, /device:TPU:0, one launch (start us, length us, event | category | flops | bytes accessed | tf_op | source)
XLA Modules:
  0.0 87.5 jit_solution(14616199292241779095)
XLA Ops:
  0.0 85.2 %shard_map.64 = bf16[256,2048]{1,0:T(8,128)(2,1)} custom-call(s32[4,16]{1,0:T(4,128)} %table.1, s32[4,1,256]{2,1,0:T(1,128)} %bitcast.3, bf16[4,64,2048]{2,1,0:T(8,128)(2,1)} %bitcast.2, bf16[2048,2048]{1,0:T(8,128)(2,1)} %w_hbm.1, bf16[64,16,2048]{2,1,0:T(8,128)(2,1)} %down_hbm.1, bf16[64,16,2048]{2,1,0:T(8,128)(2,1)} %up_hbm.1), custom_call_target="tpu_custom_call" | custom-call | tf_op jit(solution)/shard_map/pallas_call | solution.py:308
  85.2 2.3 %copy.8 = bf16[256,2048]{1,0:T(8,128)(2,1)} copy(bf16[256,2048]{1,0:T(8,128)(2,1)} %shard_map.64) | data formatting | bytes 2097152

commit v2 on v1

--- a/solution.py
+++ b/solution.py
@@ -18,10 +18,10 @@
     table, slots, x_hbm, w_hbm, down_hbm, up_hbm,
     out,
     x_all, w_all, down, up, down_sel, up_send, up_got,
-    share_out, share_got, rank_out, rank_got, fin_out, fin_got, delta,
+    share_out, share_got, rank_out, rank_got, fin_out, fin_got, delta, far_sel,
     load_sem, x_right_sem, x_left_sem, x_recv_sem,
     up_send_sem, up_recv_sem, share_send_sem, share_recv_sem,
-    rank_send_sem, rank_recv_sem, fin_send_sem, fin_recv_sem,
+    rank_send_sem, rank_recv_sem, fin_send_sem, fin_recv_sem, far_sem,
 ):
     z = lax.axis_index("replica")
     t = lax.axis_index("tensor")
@@ -108,6 +108,27 @@
             index = jnp.clip(table[g, z * cap + j] - z * owned, 0, owned - 1)
             down_sel[g, j * rank : (j + 1) * rank, :] = down[index]
 
+    last = groups - 1
+    at_end = (z == 0) | (z == last)
+
+    def far_copy(g, target):
+        return pltpu.make_async_remote_copy(
+            src_ref=down_sel.at[g],
+            dst_ref=far_sel,
+            send_sem=far_sem.at[0],
+            recv_sem=far_sem.at[1],
+            device_id={"replica": target},
+            device_id_type=MESH,
+        )
+
+    @pl.when(z == 0)
+    def _():
+        far_copy(last, 1).start()
+
+    @pl.when(z == last)
+    def _():
+        far_copy(0, last - 1).start()
+
     for copy in loads[2:]:
         copy.wait()
 
@@ -131,26 +152,46 @@
             device_id_type=MESH,
         )
 
+    def put_rank(g, total):
+        @pl.when(g == t)
+        def _():
+            rank_got[t] = total
+
+        @pl.when(g != t)
+        def _():
+            rank_out[g] = total
+            rank_copy(g).start()
+
+    def rank_terms(factors, g, owner):
+        block = x_all[g].reshape(chunks * rows, width)
+        terms = lax.dot_general(
+            factors, block, (((1,), (1,)), ((), ())), preferred_element_type=jnp.float32
+        )
+        slot = slots[g]
+        total = jnp.zeros((rank, chunks * rows), jnp.float32)
+        for j in range(cap):
+            total += jnp.where(slot == owner * cap + j, terms[j * rank : (j + 1) * rank, :], 0.0)
+        return total
+
+    @pl.when(at_end)
+    def _():
+        put_rank(last - z, jnp.zeros((rank, chunks * rows), jnp.float32))
+
     def work(g, c):
-        @pl.when(c == chunks - 1)
-        def _():
-            block = x_all[g].reshape(chunks * rows, width)
-            terms = lax.dot_general(
-                down_sel[g], block, (((1,), (1,)), ((), ())), preferred_element_type=jnp.float32
+        beside = ((z == 1) & (g == last)) | ((z == last - 1) & (g == 0))
+        done = (c == chunks - 1) & ~(at_end & (g == last - z))
+
+        @pl.when(done & ~beside)
+        def _():
+            put_rank(g, rank_terms(down_sel[g], g, z))
+
+        @pl.when(done & beside)
+        def _():
+            far_copy(0, z).wait_recv()
+            put_rank(
+                g,
+                rank_terms(down_sel[g], g, z) + rank_terms(far_sel[...], g, last - g),
             )
-            slot = slots[g]
-            total = jnp.zeros((rank, chunks * rows), jnp.float32)
-            for j in range(cap):
-                total += jnp.where(slot == z * cap + j, terms[j * rank : (j + 1) * rank, :], 0.0)
-
-            @pl.when(g == t)
-            def _():
-                rank_got[t] = total
-
-            @pl.when(g != t)
-            def _():
-                rank_out[g] = total
-                rank_copy(g).start()
 
         @pl.loop(0, tiles)
         def _(i):
@@ -171,8 +212,7 @@
     def _(c):
         work(z, c)
 
-    @pl.loop(0, (groups - 1) * chunks)
-    def _(e):
+    def event(e):
         s = e // chunks + 1
         c = lax.rem(e, chunks)
         low, high = z - s, z + s
@@ -200,6 +240,10 @@
             @pl.when((g >= 0) & (g < groups))
             def _():
                 work(g, c)
+
+    @pl.loop(0, (groups - 2) * chunks)
+    def _(e):
+        event(e)
 
     for d in range(1, peers):
         src = lax.rem(t + d, peers)
@@ -222,6 +266,11 @@
 
     for d in range(1, groups):
         fin_copy(d).start()
+
+    @pl.loop((groups - 2) * chunks, (groups - 1) * chunks - 1)
+    def _(e):
+        event(e)
+
     for d in range(1, peers):
         src = lax.rem(t + d, peers)
         pltpu.make_async_copy(up_got.at[src], up_got.at[src], up_recv_sem.at[src]).wait()
@@ -242,7 +291,7 @@
             spread, factors, (((0,), (0,)), ((), ())), preferred_element_type=jnp.float32
         )
 
-    for c in range(chunks):
+    def combine(c):
         for i in range(tiles):
             for d in range(1, peers):
                 src = lax.rem(t + d, peers)
@@ -256,6 +305,16 @@
                 base + delta[i, c * rows : (c + 1) * rows, :]
             ).astype(jnp.bfloat16)
 
+    for c in range(chunks - 2):
+        combine(c)
+
+    @pl.loop((groups - 1) * chunks - 1, (groups - 1) * chunks)
+    def _(e):
+        event(e)
+
+    for c in range(chunks - 2, chunks):
+        combine(c)
+
     @pl.loop(0, groups)
     def _(g):
         @pl.loop(0, chunks)
@@ -277,6 +336,10 @@
         def _():
             rank_copy(g).wait_send()
             up_copy(g).wait_send()
+
+    @pl.when(at_end)
+    def _():
+        far_copy(0, z).wait_send()
 
     for d in range(1, groups):
         fin_copy(d).wait_send()
@@ -307,7 +370,7 @@
     vmem = pl.BlockSpec(memory_space=pltpu.VMEM)
     return pl.pallas_call(
         functools.partial(kernel, groups, peers, chunks, tiles),
-        out_shape=jax.ShapeDtypeStruct((row_count, columns), bf16),
+        out_shape=pltpu.VMEM((row_count, columns), bf16),
         in_specs=[pl.BlockSpec(memory_space=pltpu.SMEM), vmem, hbm, hbm, hbm, hbm],
         out_specs=vmem,
         scratch_shapes=[
@@ -325,6 +388,7 @@
             pltpu.VMEM((rank, row_count), bf16),
             pltpu.VMEM((groups, rank, row_count), bf16),
             pltpu.VMEM((tiles, row_count, span), jnp.float32),
+            pltpu.VMEM((slot_rows, width), bf16),
             dma((3 + tiles,)),
             dma((groups, chunks)),
             dma((groups, chunks)),
@@ -337,6 +401,7 @@
             dma((peers,)),
             dma((groups,)),
             dma((groups,)),
+            dma((2,)),
         ],
         compiler_params=pltpu.CompilerParams(
             collective_id=0, has_side_effects=True, vmem_limit_bytes=56 * 1024 * 1024

time: 87.7 us -> 85.7 us (0.977)
  local copies, waits for them, and re-layouts: 2.3 us -> 0.97 us
    unnamed x1, local copies, waits for them, and re-layouts: 2.3 us -> 0.97 us
where the time goes in v2:
time: 85.7 us; the launch traced here: 85.5 us
  Pallas kernels  84.6 us (99%)
  local copies, waits for them, and re-layouts  0.97 us (1%)
    pallas_call x1, Pallas kernels, per_device(): pl.pallas_call(functools.partial(kernel, groups, peers, chunks, tiles), o...  84.6 us

profile of v2, /device:TPU:0, one launch (start us, length us, event | category | flops | bytes accessed | tf_op | source)
XLA Modules:
  0.0 85.5 jit_solution(9032965546999483460)
XLA Ops:
  0.0 84.6 %shard_map.64 = bf16[256,2048]{1,0:T(8,128)(2,1)S(1)} custom-call(s32[4,16]{1,0:T(4,128)} %table.1, s32[4,1,256]{2,1,0:T(1,128)} %bitcast.3, bf16[4,64,2048]{2,1,0:T(8,128)(2,1)} %bitcast.2, bf16[2048,2048]{1,0:T(8,128)(2,1)} %w_hbm.1, bf16[64,16,2048]{2,1,0:T(8,128)(2,1)} %down_hbm.1, bf16[64,16,2048]{2,1,0:T(8,128)(2,1)} %up_hbm.1), custom_call_target="tpu_custom_call" | custom-call | tf_op jit(solution)/shard_map/pallas_call | solution.py:371
  84.6 1.0 %copy.8 = bf16[256,2048]{1,0:T(8,128)(2,1)} copy(bf16[256,2048]{1,0:T(8,128)(2,1)S(1)} %shard_map.64) | data formatting | bytes 2097152

commit v3 on v2

--- a/solution.py
+++ b/solution.py
@@ -10,7 +10,7 @@
 MESH = pl.DeviceIdType.MESH
 adapter_scale = 2.0
 row_chunk = 64
-tile_width = 1024
+tile_width = 2048
 
 
 def kernel(
@@ -21,7 +21,7 @@
     share_out, share_got, rank_out, rank_got, fin_out, fin_got, delta, far_sel,
     load_sem, x_right_sem, x_left_sem, x_recv_sem,
     up_send_sem, up_recv_sem, share_send_sem, share_recv_sem,
-    rank_send_sem, rank_recv_sem, fin_send_sem, fin_recv_sem, far_sem,
+    rank_send_sem, rank_recv_sem, fin_send_sem, fin_recv_sem, far_sem, half_sem,
 ):
     z = lax.axis_index("replica")
     t = lax.axis_index("tensor")
@@ -65,6 +65,20 @@
             device_id_type=MESH,
         )
 
+    half = rows // 2
+    tail = chunks - 1
+
+    def x_half(g, step, h):
+        sems = x_right_sem if step > 0 else x_left_sem
+        return pltpu.make_async_remote_copy(
+            src_ref=x_all.at[g, tail, pl.ds(h * half, half)],
+            dst_ref=x_all.at[g, tail, pl.ds(h * half, half)],
+            send_sem=sems.at[g, tail],
+            recv_sem=half_sem.at[h],
+            device_id={"replica": z + step},
+            device_id_type=MESH,
+        )
+
     for c in range(chunks):
         @pl.when(z < groups - 1)
         def _():
@@ -221,17 +235,31 @@
         def _():
             x_copy(x_hbm.at[0], low, c, 1).wait_recv()
 
-            @pl.when(z < groups - 1)
+            split = (c == tail) & (z == last - 1) & (low == 0)
+
+            @pl.when((z < last) & ~split)
             def _():
                 x_copy(x_all.at[low, c], low, c, 1).start()
 
+            @pl.when(split)
+            def _():
+                for h in range(2):
+                    x_half(low, 1, h).start()
+
         @pl.when(high < groups)
         def _():
             x_copy(x_hbm.at[0], high, c, -1).wait_recv()
 
-            @pl.when(z > 0)
+            split = (c == tail) & (z == 1) & (high == last)
+
+            @pl.when((z > 0) & ~split)
             def _():
                 x_copy(x_all.at[high, c], high, c, -1).start()
+
+            @pl.when(split)
+            def _():
+                for h in range(2):
+                    x_half(high, -1, h).start()
 
         @pl.loop(0, 2)
         def _(side):
@@ -308,9 +336,37 @@
     for c in range(chunks - 2):
         combine(c)
 
-    @pl.loop((groups - 1) * chunks - 1, (groups - 1) * chunks)
-    def _(e):
-        event(e)
+    def half_share(g, i, h):
+        return pltpu.make_async_remote_copy(
+            src_ref=share_out.at[g, tail, i, pl.ds(h * half, half)],
+            dst_ref=share_got.at[t, tail, i, pl.ds(h * half, half)],
+            send_sem=share_send_sem.at[g, tail, i],
+            recv_sem=share_recv_sem.at[t, tail, i],
+            device_id={"tensor": g},
+            device_id_type=MESH,
+        )
+
+    @pl.when(at_end)
+    def _():
+        g = last - z
+        for h in range(2):
+            x_half(g, 1, h).wait_recv()
+            part = slice(h * half, (h + 1) * half)
+
+            @pl.loop(0, tiles)
+            def _(i):
+                share = jnp.dot(
+                    x_all[g, tail, part, :], w_all[i], preferred_element_type=jnp.float32
+                ).astype(jnp.bfloat16)
+
+                @pl.when(g == t)
+                def _():
+                    share_got[t, tail, i, part, :] = share
+
+                @pl.when(g != t)
+                def _():
+                    share_out[g, tail, i, part, :] = share
+                    half_share(g, i, h).start()
 
     for c in range(chunks - 2, chunks):
         combine(c)
@@ -402,6 +458,7 @@
             dma((groups,)),
             dma((groups,)),
             dma((2,)),
+            dma((2,)),
         ],
         compiler_params=pltpu.CompilerParams(
             collective_id=0, has_side_effects=True, vmem_limit_bytes=56 * 1024 * 1024

time: 85.7 us -> 86.2 us (level)
  no operation moved by 1% of the time
where the time goes in v3:
time: 86.2 us; the launch traced here: 86 us
  Pallas kernels  85 us (99%)
  local copies, waits for them, and re-layouts  0.97 us (1%)
    pallas_call x1, Pallas kernels, per_device(): pl.pallas_call(functools.partial(kernel, groups, peers, chunks, tiles), o...  85 us

profile of v3, /device:TPU:0, one launch (start us, length us, event | category | flops | bytes accessed | tf_op | source)
XLA Modules:
  0.0 86.0 jit_solution(1018575663521794880)
XLA Ops:
  0.0 85.0 %shard_map.64 = bf16[256,2048]{1,0:T(8,128)(2,1)S(1)} custom-call(s32[4,16]{1,0:T(4,128)} %table.1, s32[4,1,256]{2,1,0:T(1,128)} %bitcast.3, bf16[4,64,2048]{2,1,0:T(8,128)(2,1)} %bitcast.2, bf16[2048,2048]{1,0:T(8,128)(2,1)} %w_hbm.1, bf16[64,16,2048]{2,1,0:T(8,128)(2,1)} %down_hbm.1, bf16[64,16,2048]{2,1,0:T(8,128)(2,1)} %up_hbm.1), custom_call_target="tpu_custom_call" | custom-call | tf_op jit(solution)/shard_map/pallas_call | solution.py:427
  85.0 1.0 %copy.8 = bf16[256,2048]{1,0:T(8,128)(2,1)} copy(bf16[256,2048]{1,0:T(8,128)(2,1)S(1)} %shard_map.64) | data formatting | bytes 2097152
